TPU v7x, 32 devices: a whole 2x2x4 slice. The times are simulated.
32 devices in a mesh: groups: 2 (over y), rows: 4 (over z), chan: 4 (over x, core).
Axes of the slice: x: 2, y: 2, z: 4, core: 2. Of those that a mesh axis runs over, the one named last changes fastest.
Arguments:
- pair_act: bfloat16 [512, 256, 128], P(('groups', 'chan'), 'rows'), parts along dimension 0, may hold values from -6 to 6
- pair_mask: int32 [512, 256], P(('groups', 'chan'), 'rows'), parts along dimension 0, may hold values 0 or 1
- input_gain: float32 [2, 128], replicated, may hold values from 0.5 to 1.5
- input_bias: float32 [2, 128], replicated, may hold values from -3 to 3
- proj_weight: bfloat16 [2, 128, 4, 128], replicated, may hold values from -0.5 to 0.5
- gate_weight: bfloat16 [2, 128, 128], replicated, may hold values from -0.5 to 0.5
- output_gain: float32 [2, 128], replicated, may hold values from 0.5 to 1.5
- output_bias: float32 [2, 128], replicated, may hold values from -3 to 3
- out_weight: bfloat16 [2, 128, 128], replicated, may hold values from -0.5 to 0.5
Outputs:
- pair_out: bfloat16 [512, 256, 128], P(('groups', 'chan'), 'rows'), parts along dimension 0
There are 2 independent parts, one for each index of `groups`. A program takes and returns all parts, laid end to end along the dimension named above; an argument that names none is the same for every part. Nothing has to cross between parts.
All inputs are finite; a program needn't handle non-finite values. No bound on the sum of `pair_mask` on one device may be relied on, other than what follows from the above.
Results may differ from a plain program's by a relative error of at most 0.0075.
Values may be sent and summed in bfloat16 or wider, within the bound.
A program may use at most 64 MiB of HBM per device.

v0:
```python
import functools

import jax
import jax.numpy as jnp
from jax import lax
from jax.experimental import pallas as pl
from jax.experimental.pallas import tpu as pltpu
from jax.sharding import PartitionSpec as P


def layer_norm(values, norm_gain, norm_bias):
    center = values - jnp.mean(values, axis=-1, keepdims=True)
    spread = jnp.mean(center * center, axis=-1, keepdims=True)
    return center * lax.rsqrt(spread + 1e-05) * norm_gain + norm_bias


def outgoing_sum(left_split, right_split):
    return jnp.einsum(
        "cik,cjk->cij",
        left_split,
        lax.all_gather(right_split, "chan", axis=1, tiled=True),
        preferred_element_type=jnp.float32,
    )


def incoming_sum(left_split, right_split):
    summed = lax.psum_scatter(
        jnp.einsum(
            "cki,ckj->icj", left_split, right_split, preferred_element_type=jnp.float32
        ).astype(jnp.bfloat16),
        "chan",
        scatter_dimension=0,
        tiled=True,
    ).astype(jnp.float32)
    return jnp.transpose(summed, (1, 0, 2))


def output_mix(combined, layer_index, output_gain, output_bias, out_weight):
    pixels = lax.all_to_all(combined, "rows", split_axis=2, concat_axis=0, tiled=True)
    values = pixels.astype(jnp.float32)
    center = values - jnp.mean(values, axis=0, keepdims=True)
    spread = jnp.mean(center * center, axis=0, keepdims=True)
    normed_out = (
        center * lax.rsqrt(spread + 1e-05) * output_gain[layer_index][:, None, None]
        + output_bias[layer_index][:, None, None]
    ).astype(jnp.bfloat16)
    return jnp.einsum(
        "cij,cd->ijd", normed_out, out_weight[layer_index], preferred_element_type=jnp.float32
    )


def tri_layer(
    pair_now,
    mask_float,
    layer_index,
    incoming,
    input_gain,
    input_bias,
    proj_weight,
    gate_weight,
    output_gain,
    output_bias,
    out_weight,
):
    normed_in = layer_norm(
        pair_now.astype(jnp.float32), input_gain[layer_index], input_bias[layer_index]
    ).astype(jnp.bfloat16)
    projected = jnp.einsum(
        "ijd,dhc->hcij", normed_in, proj_weight[layer_index], preferred_element_type=jnp.float32
    )
    left_edge = (jax.nn.sigmoid(projected[1]) * projected[0] * mask_float[None]).astype(
        jnp.bfloat16
    )
    right_edge = (jax.nn.sigmoid(projected[3]) * projected[2] * mask_float[None]).astype(
        jnp.bfloat16
    )
    gating = jax.nn.sigmoid(
        jnp.einsum(
            "ijd,de->ije", normed_in, gate_weight[layer_index], preferred_element_type=jnp.float32
        )
    )
    left_split, right_split = (
        lax.all_to_all(left_edge, "rows", split_axis=0, concat_axis=2, tiled=True),
        lax.all_to_all(right_edge, "rows", split_axis=0, concat_axis=2, tiled=True),
    )
    if incoming:
        combined = incoming_sum(left_split, right_split)
    else:
        combined = outgoing_sum(left_split, right_split)
    combined = lax.optimization_barrier(combined.astype(jnp.bfloat16))
    mixed_out = output_mix(combined, layer_index, output_gain, output_bias, out_weight)
    return lax.optimization_barrier(
        (pair_now.astype(jnp.float32) + gating * mixed_out).astype(jnp.bfloat16)
    )


def on_device(
    pair_act,
    pair_mask,
    input_gain,
    input_bias,
    proj_weight,
    gate_weight,
    output_gain,
    output_bias,
    out_weight,
):
    mask_float = pair_mask.astype(jnp.float32)
    after_out = tri_layer(
        pair_act,
        mask_float,
        0,
        False,
        input_gain,
        input_bias,
        proj_weight,
        gate_weight,
        output_gain,
        output_bias,
        out_weight,
    )
    return tri_layer(
        after_out,
        mask_float,
        1,
        True,
        input_gain,
        input_bias,
        proj_weight,
        gate_weight,
        output_gain,
        output_bias,
        out_weight,
    )


def sigmoid(values):
    return 0.5 * jnp.tanh(0.5 * values) + 0.5


def swap_halves(low, high):
    half = low.shape[-1] // 2
    lane = lax.broadcasted_iota(jnp.int32, low.shape, low.ndim - 1)
    axis = low.ndim - 1
    first = jnp.where(lane < half, low, pltpu.roll(high, half, axis))
    second = jnp.where(lane < half, pltpu.roll(low, half, axis), high)
    return first, second


def fused_kernel(
    rows,
    chan,
    pair_ref,
    mask_ref,
    in_gain_ref,
    in_bias_ref,
    proj_ref,
    gate_w_ref,
    out_gain_ref,
    out_bias_ref,
    out_w_ref,
    out_ref,
    mid_ref,
    left_wide,
    right_wide,
    gate_buf,
    edge_send,
    edge_recv,
    sum_send,
    sum_recv,
    edge_ssem,
    edge_rsem,
    sum_ssem,
    sum_rsem,
):
    peers = rows * chan
    my_row = lax.axis_index("rows")
    my_chan = lax.axis_index("chan")
    me = my_chan * rows + my_row
    side = pair_ref.shape[1]
    width = pair_ref.shape[2]
    half = pair_ref.shape[0] // 2
    own = edge_send.shape[3]
    lanes = 2 * side

    def coords(peer):
        return {"rows": lax.rem(peer, rows), "chan": lax.div(peer, rows)}

    barrier = pltpu.get_barrier_semaphore()

    @pl.loop(1, peers)
    def _(step):
        peer = lax.rem(me + step, peers)
        pl.semaphore_signal(
            barrier, inc=1, device_id=coords(peer), device_id_type=pl.DeviceIdType.MESH
        )

    def edge_copy(u, step, peer):
        return pltpu.make_async_remote_copy(
            src_ref=edge_send.at[u, peer],
            dst_ref=edge_recv.at[u, me],
            send_sem=edge_ssem.at[u, step],
            recv_sem=edge_rsem.at[u, step],
            device_id=coords(peer),
            device_id_type=pl.DeviceIdType.MESH,
        )

    def sum_copy(u, step, peer):
        return pltpu.make_async_remote_copy(
            src_ref=sum_send.at[u, peer],
            dst_ref=sum_recv.at[u, me],
            send_sem=sum_ssem.at[u, step],
            recv_sem=sum_rsem.at[u, step],
            device_id=coords(peer),
            device_id_type=pl.DeviceIdType.MESH,
        )

    for u in range(2):
        source = pair_ref if u == 0 else mid_ref
        target = mid_ref if u == 0 else out_ref

        @pl.loop(0, half)
        def _(ip):
            cells = jnp.concatenate([source[ip], source[ip + half]], axis=0).astype(jnp.float32)
            center = cells - jnp.mean(cells, axis=-1, keepdims=True)
            spread = jnp.mean(center * center, axis=-1, keepdims=True)
            normed = (
                center * lax.rsqrt(spread + 1e-05) * in_gain_ref[u : u + 1, :]
                + in_bias_ref[u : u + 1, :]
            ).astype(jnp.bfloat16)
            projected = lax.dot_general(
                proj_ref[u], normed, (((1,), (1,)), ((), ())), preferred_element_type=jnp.float32
            )
            mask_row = mask_ref[pl.ds(ip, 1), :]
            left = sigmoid(projected[width : 2 * width]) * projected[:width] * mask_row
            right = sigmoid(projected[3 * width :]) * projected[2 * width : 3 * width] * mask_row
            left_wide[:, pl.ds(ip, 1), :] = left[:, None, :]
            right_wide[:, pl.ds(ip, 1), :] = right[:, None, :]
            gate_buf[ip] = sigmoid(
                jnp.dot(normed, gate_w_ref[u], preferred_element_type=jnp.float32)
            )

        if u == 0:
            pl.semaphore_wait(barrier, peers - 1)

        @pl.loop(1, peers)
        def _(step):
            peer = lax.rem(me + step, peers)
            edge_send[u, peer, 0] = left_wide[pl.ds(peer * own, own)].astype(jnp.bfloat16)
            edge_send[u, peer, 1] = right_wide[pl.ds(peer * own, own)].astype(jnp.bfloat16)
            edge_copy(u, step, peer).start()

        edge_recv[u, me, 0] = left_wide[pl.ds(me * own, own)].astype(jnp.bfloat16)
        edge_recv[u, me, 1] = right_wide[pl.ds(me * own, own)].astype(jnp.bfloat16)

        @pl.loop(1, peers)
        def _(step):
            edge_copy(u, step, lax.rem(me + step, peers)).wait()

        @pl.loop(0, own)
        def _(c):
            def whole(kind):
                pieces = []
                for a in range(chan):
                    first, second = [], []
                    for r in range(0, rows, 2):
                        low = edge_recv[u, a * rows + r, kind, c].astype(jnp.float32)
                        high = edge_recv[u, a * rows + r + 1, kind, c].astype(jnp.float32)
                        one, two = swap_halves(low, high)
                        first.append(one)
                        second.append(two)
                    pieces.append(jnp.concatenate(first, axis=1))
                    pieces.append(jnp.concatenate(second, axis=1))
                return jnp.concatenate(pieces, axis=0).astype(jnp.bfloat16)

            left = whole(0)
            right = whole(1)
            depth = 1 if u == 0 else 0
            summed = lax.dot_general(
                left,
                right,
                (((depth,), (depth,)), ((), ())),
                preferred_element_type=jnp.float32,
            )
            for a in range(chan):
                for r in range(0, rows, 2):
                    top = 2 * half * a
                    upper = summed[top : top + half, r * side : r * side + lanes]
                    lower = summed[top + half : top + 2 * half, r * side : r * side + lanes]
                    one, two = swap_halves(upper, lower)
                    sum_send[u, a * rows + r, c] = one.astype(jnp.bfloat16)
                    sum_send[u, a * rows + r + 1, c] = two.astype(jnp.bfloat16)

        @pl.loop(1, peers)
        def _(step):
            sum_copy(u, step, lax.rem(me + step, peers)).start()

        left_wide[pl.ds(me * own, own)] = sum_send[u, me].astype(jnp.float32)

        @pl.loop(1, peers)
        def _(step):
            sum_copy(u, step, lax.rem(me + step, peers)).wait()
            peer = lax.rem(me + peers - step, peers)
            left_wide[pl.ds(peer * own, own)] = sum_recv[u, peer].astype(jnp.float32)

        @pl.loop(0, half)
        def _(ip):
            values = left_wide[:, pl.ds(ip, 1), :].reshape(width, lanes)
            center = values - jnp.mean(values, axis=0, keepdims=True)
            spread = jnp.mean(center * center, axis=0, keepdims=True)
            normed = (
                center * lax.rsqrt(spread + 1e-05) * out_gain_ref[u] + out_bias_ref[u]
            ).astype(jnp.bfloat16)
            mixed = lax.dot_general(
                normed,
                out_w_ref[u],
                (((0,), (0,)), ((), ())),
                preferred_element_type=jnp.float32,
            )
            moved = gate_buf[ip] * mixed
            target[ip] = (source[ip].astype(jnp.float32) + moved[:side]).astype(jnp.bfloat16)
            target[ip + half] = (
                source[ip + half].astype(jnp.float32) + moved[side:]
            ).astype(jnp.bfloat16)


def fused_on_device(rows, chan):
    def run(
        pair_act,
        pair_mask,
        input_gain,
        input_bias,
        proj_weight,
        gate_weight,
        output_gain,
        output_bias,
        out_weight,
    ):
        first, side, width = pair_act.shape
        half = first // 2
        hidden = proj_weight.shape[-1]
        peers = rows * chan
        own = hidden // peers
        lanes = 2 * side
        mask_float = pair_mask.astype(jnp.float32)
        mask_rows = jnp.concatenate([mask_float[:half], mask_float[half:]], axis=1)
        proj_flat = jnp.transpose(proj_weight, (0, 2, 3, 1)).reshape(2, 4 * hidden, width)
        vmem = pl.BlockSpec(memory_space=pltpu.VMEM)
        return pl.pallas_call(
            functools.partial(fused_kernel, rows, chan),
            out_shape=jax.ShapeDtypeStruct(pair_act.shape, jnp.bfloat16),
            in_specs=[vmem] * 9,
            out_specs=vmem,
            scratch_shapes=[
                pltpu.VMEM((first, side, width), jnp.bfloat16),
                pltpu.VMEM((hidden, half, lanes), jnp.float32),
                pltpu.VMEM((hidden, half, lanes), jnp.float32),
                pltpu.VMEM((half, lanes, width), jnp.float32),
                pltpu.VMEM((2, peers, 2, own, half, lanes), jnp.bfloat16),
                pltpu.VMEM((2, peers, 2, own, half, lanes), jnp.bfloat16),
                pltpu.VMEM((2, peers, own, half, lanes), jnp.bfloat16),
                pltpu.VMEM((2, peers, own, half, lanes), jnp.bfloat16),
                pltpu.SemaphoreType.DMA((2, peers)),
                pltpu.SemaphoreType.DMA((2, peers)),
                pltpu.SemaphoreType.DMA((2, peers)),
                pltpu.SemaphoreType.DMA((2, peers)),
            ],
            compiler_params=pltpu.CompilerParams(
                collective_id=0, has_side_effects=True, vmem_limit_bytes=48 * 1024 * 1024
            ),
        )(
            pair_act,
            mask_rows,
            input_gain,
            input_bias,
            proj_flat,
            gate_weight,
            output_gain[:, :, None],
            output_bias[:, :, None],
            out_weight,
        )

    return run


def solution(mesh):
    in_specs = (
        P(("groups", "chan"), "rows", None),
        P(("groups", "chan"), "rows"),
        P(),
        P(),
        P(),
        P(),
        P(),
        P(),
        P(),
    )
    out_specs = P(("groups", "chan"), "rows", None)
    rows, chan = mesh.shape["rows"], mesh.shape["chan"]
    fused = fused_on_device(rows, chan)

    def choose(pair_act, pair_mask, *parameters):
        hidden = parameters[2].shape[-1]
        fits = (
            pair_act.shape[1] == 64
            and pair_act.shape[0] % 32 == 0
            and rows % 2 == 0
            and hidden % (rows * chan) == 0
        )
        body = fused if fits else on_device
        return body(pair_act, pair_mask, *parameters)

    return jax.shard_map(
        choose, mesh=mesh, in_specs=in_specs, out_specs=out_specs, check_vma=False
    )
```

profile of v0, /device:TPU:0, one launch (start us, length us, event | category | flops | bytes accessed | tf_op | source)
XLA Modules:
  0.0 205.2 jit_solution(17796556337612696204)
XLA Ops:
  0.0 0.0 copy-start.5
  0.0 0.8 convert_element_type.3
  0.8 0.1 pad_maximum_fusion.mask_ref
  0.9 0.0 copy-start.6
  0.9 0.8 copy.12.out_gain_ref
  1.7 0.0 copy-done.6
  1.7 0.1 copy.13.out_bias_ref
  1.9 0.0 copy-done.5
  1.9 0.0 copy-start.1
  1.9 0.0 copy-start.2
  1.9 0.0 copy-start.4
  1.9 0.2 copy.11
  2.1 0.0 copy-start.3
  2.1 0.6 copy-done.1
  2.7 0.0 copy-done.2
  2.8 0.0 copy-done.4
  2.8 0.1 copy-done.3
  2.8 0.0 copy-start
  2.8 1.2 copy-done
  4.0 200.2 %shard_map.91 = bf16[64,64,128]{2,1,0:T(8,128)(2,1)S(1)} custom-call(bf16[64,64,128]{2,1,0:T(8,128)(2,1)S(1)} %copy-done, f32[32,128]{1,0:T(8,128)S(1)} %pad_maximum_fusion.mask_ref, f32[2,128]{1,0:T(2,128)S(1)} %copy-done.3, f32[2,128]{1,0:T(2,128)S(1)} %copy-done.4, bf16[2,512,128]{2,1,0:T(8,128)(2,1)S(1)} %bitcast.4, bf16[2,128,128]{2,1,0:T(8,128)(2,1)S(1)} %copy-done.1, ...), custom_call_target="tpu_custom_call" | custom-call | tf_op jit(solution)/shard_map/pallas_call | solution.py:349
  204.2 1.0 copy.15
  (1 shorter events, 0.0 us)
Async XLA Ops:
  0.0 1.9 copy-start.5
  0.9 0.8 copy-start.6
  1.9 0.8 copy-start.1
  1.9 0.9 copy-start.2
  1.9 0.9 copy-start.4
  2.1 0.7 copy-start.3
  2.8 1.2 copy-start
where the time goes:
time: 206 us; the launch traced here: 205 us
  Pallas kernels  200 us (97%)
  local copies, waits for them, and re-layouts  4.06 us (2%)
    pallas_call x1, Pallas kernels, run(): pl.pallas_call(functools.partial(fused_kernel, rows, chan), out_shape=jax...  200 us

commit v1 on v0

--- a/solution.py
+++ b/solution.py
@@ -134,6 +134,10 @@
     )
 
 
+PARTS = 2
+UNROLL = 4
+
+
 def sigmoid(values):
     return 0.5 * jnp.tanh(0.5 * values) + 0.5
 
@@ -163,6 +167,7 @@
     mid_ref,
     left_wide,
     right_wide,
+    sum_wide,
     gate_buf,
     edge_send,
     edge_recv,
@@ -180,7 +185,8 @@
     side = pair_ref.shape[1]
     width = pair_ref.shape[2]
     half = pair_ref.shape[0] // 2
-    own = edge_send.shape[3]
+    own = edge_send.shape[4]
+    depth = half // PARTS
     lanes = 2 * side
 
     def coords(peer):
@@ -195,31 +201,28 @@
             barrier, inc=1, device_id=coords(peer), device_id_type=pl.DeviceIdType.MESH
         )
 
-    def edge_copy(u, step, peer):
+    def edge_copy(u, part, step, peer):
         return pltpu.make_async_remote_copy(
-            src_ref=edge_send.at[u, peer],
-            dst_ref=edge_recv.at[u, me],
-            send_sem=edge_ssem.at[u, step],
-            recv_sem=edge_rsem.at[u, step],
+            src_ref=edge_send.at[u, part, peer],
+            dst_ref=edge_recv.at[u, part, me],
+            send_sem=edge_ssem.at[u, part, step],
+            recv_sem=edge_rsem.at[u, part, step],
             device_id=coords(peer),
             device_id_type=pl.DeviceIdType.MESH,
         )
 
-    def sum_copy(u, step, peer):
+    def sum_copy(u, part, step, peer):
         return pltpu.make_async_remote_copy(
-            src_ref=sum_send.at[u, peer],
-            dst_ref=sum_recv.at[u, me],
-            send_sem=sum_ssem.at[u, step],
-            recv_sem=sum_rsem.at[u, step],
+            src_ref=sum_send.at[u, part, peer],
+            dst_ref=sum_recv.at[u, part, me],
+            send_sem=sum_ssem.at[u, part, step],
+            recv_sem=sum_rsem.at[u, part, step],
             device_id=coords(peer),
             device_id_type=pl.DeviceIdType.MESH,
         )
 
-    for u in range(2):
-        source = pair_ref if u == 0 else mid_ref
-        target = mid_ref if u == 0 else out_ref
-
-        @pl.loop(0, half)
+    def make_edges(u, part, source):
+        @pl.loop(part * depth, (part + 1) * depth, unroll=UNROLL)
         def _(ip):
             cells = jnp.concatenate([source[ip], source[ip + half]], axis=0).astype(jnp.float32)
             center = cells - jnp.mean(cells, axis=-1, keepdims=True)
@@ -236,36 +239,46 @@
             right = sigmoid(projected[3 * width :]) * projected[2 * width : 3 * width] * mask_row
             left_wide[:, pl.ds(ip, 1), :] = left[:, None, :]
             right_wide[:, pl.ds(ip, 1), :] = right[:, None, :]
-            gate_buf[ip] = sigmoid(
+            gate_buf[u, ip] = sigmoid(
                 jnp.dot(normed, gate_w_ref[u], preferred_element_type=jnp.float32)
             )
 
-        if u == 0:
-            pl.semaphore_wait(barrier, peers - 1)
-
+    def narrow(wide, part, peer):
+        return wide[pl.ds(peer * own, own), part * depth : (part + 1) * depth, :].astype(
+            jnp.bfloat16
+        )
+
+    def send_edges(u, part):
         @pl.loop(1, peers)
         def _(step):
             peer = lax.rem(me + step, peers)
-            edge_send[u, peer, 0] = left_wide[pl.ds(peer * own, own)].astype(jnp.bfloat16)
-            edge_send[u, peer, 1] = right_wide[pl.ds(peer * own, own)].astype(jnp.bfloat16)
-            edge_copy(u, step, peer).start()
-
-        edge_recv[u, me, 0] = left_wide[pl.ds(me * own, own)].astype(jnp.bfloat16)
-        edge_recv[u, me, 1] = right_wide[pl.ds(me * own, own)].astype(jnp.bfloat16)
-
+            edge_send[u, part, peer, 0] = narrow(left_wide, part, peer)
+            edge_send[u, part, peer, 1] = narrow(right_wide, part, peer)
+            edge_copy(u, part, step, peer).start()
+
+        edge_recv[u, part, me, 0] = narrow(left_wide, part, me)
+        edge_recv[u, part, me, 1] = narrow(right_wide, part, me)
+
+    def wait_edges(u, part):
         @pl.loop(1, peers)
         def _(step):
-            edge_copy(u, step, lax.rem(me + step, peers)).wait()
-
-        @pl.loop(0, own)
+            edge_copy(u, part, step, lax.rem(me + step, peers)).wait()
+
+    def make_sums(u):
+        @pl.loop(0, own, unroll=2)
         def _(c):
             def whole(kind):
                 pieces = []
                 for a in range(chan):
                     first, second = [], []
                     for r in range(0, rows, 2):
-                        low = edge_recv[u, a * rows + r, kind, c].astype(jnp.float32)
-                        high = edge_recv[u, a * rows + r + 1, kind, c].astype(jnp.float32)
+                        low, high = (
+                            jnp.concatenate(
+                                [edge_recv[u, part, peer, kind, c] for part in range(PARTS)],
+                                axis=0,
+                            ).astype(jnp.float32)
+                            for peer in (a * rows + r, a * rows + r + 1)
+                        )
                         one, two = swap_halves(low, high)
                         first.append(one)
                         second.append(two)
@@ -275,11 +288,11 @@
 
             left = whole(0)
             right = whole(1)
-            depth = 1 if u == 0 else 0
+            over = 1 if u == 0 else 0
             summed = lax.dot_general(
                 left,
                 right,
-                (((depth,), (depth,)), ((), ())),
+                (((over,), (over,)), ((), ())),
                 preferred_element_type=jnp.float32,
             )
             for a in range(chan):
@@ -288,24 +301,32 @@
                     upper = summed[top : top + half, r * side : r * side + lanes]
                     lower = summed[top + half : top + 2 * half, r * side : r * side + lanes]
                     one, two = swap_halves(upper, lower)
-                    sum_send[u, a * rows + r, c] = one.astype(jnp.bfloat16)
-                    sum_send[u, a * rows + r + 1, c] = two.astype(jnp.bfloat16)
-
+                    for part in range(PARTS):
+                        piece = slice(part * depth, (part + 1) * depth)
+                        sum_send[u, part, a * rows + r, c] = one[piece].astype(jnp.bfloat16)
+                        sum_send[u, part, a * rows + r + 1, c] = two[piece].astype(jnp.bfloat16)
+
+    def send_sums(u, part):
         @pl.loop(1, peers)
         def _(step):
-            sum_copy(u, step, lax.rem(me + step, peers)).start()
-
-        left_wide[pl.ds(me * own, own)] = sum_send[u, me].astype(jnp.float32)
+            sum_copy(u, part, step, lax.rem(me + step, peers)).start()
+
+    def take_sums(u, part):
+        piece = slice(part * depth, (part + 1) * depth)
+        sum_wide[pl.ds(me * own, own), piece, :] = sum_send[u, part, me].astype(jnp.float32)
 
         @pl.loop(1, peers)
         def _(step):
-            sum_copy(u, step, lax.rem(me + step, peers)).wait()
+            sum_copy(u, part, step, lax.rem(me + step, peers)).wait()
             peer = lax.rem(me + peers - step, peers)
-            left_wide[pl.ds(peer * own, own)] = sum_recv[u, peer].astype(jnp.float32)
-
-        @pl.loop(0, half)
+            sum_wide[pl.ds(peer * own, own), piece, :] = sum_recv[u, part, peer].astype(
+                jnp.float32
+            )
+
+    def mix(u, part, source, target):
+        @pl.loop(part * depth, (part + 1) * depth, unroll=UNROLL)
         def _(ip):
-            values = left_wide[:, pl.ds(ip, 1), :].reshape(width, lanes)
+            values = sum_wide[:, pl.ds(ip, 1), :].reshape(width, lanes)
             center = values - jnp.mean(values, axis=0, keepdims=True)
             spread = jnp.mean(center * center, axis=0, keepdims=True)
             normed = (
@@ -317,11 +338,35 @@
                 (((0,), (0,)), ((), ())),
                 preferred_element_type=jnp.float32,
             )
-            moved = gate_buf[ip] * mixed
+            moved = gate_buf[u, ip] * mixed
             target[ip] = (source[ip].astype(jnp.float32) + moved[:side]).astype(jnp.bfloat16)
             target[ip + half] = (
                 source[ip + half].astype(jnp.float32) + moved[side:]
             ).astype(jnp.bfloat16)
+
+    for part in range(PARTS):
+        make_edges(0, part, pair_ref)
+        if part == 0:
+            pl.semaphore_wait(barrier, peers - 1)
+        send_edges(0, part)
+    for part in range(PARTS):
+        wait_edges(0, part)
+    make_sums(0)
+    for part in range(PARTS):
+        send_sums(0, part)
+    for part in range(PARTS):
+        take_sums(0, part)
+        mix(0, part, pair_ref, mid_ref)
+        make_edges(1, part, mid_ref)
+        send_edges(1, part)
+    for part in range(PARTS):
+        wait_edges(1, part)
+    make_sums(1)
+    for part in range(PARTS):
+        send_sums(1, part)
+    for part in range(PARTS):
+        take_sums(1, part)
+        mix(1, part, mid_ref, out_ref)
 
 
 def fused_on_device(rows, chan):
@@ -355,15 +400,16 @@
                 pltpu.VMEM((first, side, width), jnp.bfloat16),
                 pltpu.VMEM((hidden, half, lanes), jnp.float32),
                 pltpu.VMEM((hidden, half, lanes), jnp.float32),
-                pltpu.VMEM((half, lanes, width), jnp.float32),
-                pltpu.VMEM((2, peers, 2, own, half, lanes), jnp.bfloat16),
-                pltpu.VMEM((2, peers, 2, own, half, lanes), jnp.bfloat16),
-                pltpu.VMEM((2, peers, own, half, lanes), jnp.bfloat16),
-                pltpu.VMEM((2, peers, own, half, lanes), jnp.bfloat16),
-                pltpu.SemaphoreType.DMA((2, peers)),
-                pltpu.SemaphoreType.DMA((2, peers)),
-                pltpu.SemaphoreType.DMA((2, peers)),
-                pltpu.SemaphoreType.DMA((2, peers)),
+                pltpu.VMEM((hidden, half, lanes), jnp.float32),
+                pltpu.VMEM((2, half, lanes, width), jnp.float32),
+                pltpu.VMEM((2, PARTS, peers, 2, own, half // PARTS, lanes), jnp.bfloat16),
+                pltpu.VMEM((2, PARTS, peers, 2, own, half // PARTS, lanes), jnp.bfloat16),
+                pltpu.VMEM((2, PARTS, peers, own, half // PARTS, lanes), jnp.bfloat16),
+                pltpu.VMEM((2, PARTS, peers, own, half // PARTS, lanes), jnp.bfloat16),
+                pltpu.SemaphoreType.DMA((2, PARTS, peers)),
+                pltpu.SemaphoreType.DMA((2, PARTS, peers)),
+                pltpu.SemaphoreType.DMA((2, PARTS, peers)),
+                pltpu.SemaphoreType.DMA((2, PARTS, peers)),
             ],
             compiler_params=pltpu.CompilerParams(
                 collective_id=0, has_side_effects=True, vmem_limit_bytes=48 * 1024 * 1024
@@ -403,7 +449,7 @@
         hidden = parameters[2].shape[-1]
         fits = (
             pair_act.shape[1] == 64
-            and pair_act.shape[0] % 32 == 0
+            and pair_act.shape[0] % (32 * PARTS) == 0
             and rows % 2 == 0
             and hidden % (rows * chan) == 0
         )

time: 206 us -> 160 us (0.78)
  Pallas kernels: 200 us -> 155 us
    pallas_call x1, Pallas kernels: 200 us -> 155 us  [run(): pl.pallas_call(functools.partial(fused_kernel, rows, chan), out_shape=jax...]
where the time goes in v1:
time: 160 us
  Pallas kernels  155 us (97%)
  local copies, waits for them, and re-layouts  4.06 us (3%)
    pallas_call x1, Pallas kernels, run(): pl.pallas_call(functools.partial(fused_kernel, rows, chan), out_shape=jax...  155 us

profile of v1, /device:TPU:0, one launch (start us, length us, event | category | flops | bytes accessed | tf_op | source)
XLA Modules:
  0.0 160.0 jit_solution(16847405329400668151)
XLA Ops:
  0.0 0.0 copy-start.5
  0.0 0.8 convert_element_type.3
  0.8 0.1 pad_maximum_fusion.mask_ref
  0.9 0.0 copy-start.6
  0.9 0.8 copy.12.out_gain_ref
  1.7 0.0 copy-done.6
  1.7 0.1 copy.13.out_bias_ref
  1.9 0.0 copy-done.5
  1.9 0.0 copy-start.1
  1.9 0.0 copy-start.2
  1.9 0.0 copy-start.4
  1.9 0.2 copy.11
  2.1 0.0 copy-start.3
  2.1 0.6 copy-done.1
  2.7 0.0 copy-done.2
  2.8 0.0 copy-done.4
  2.8 0.1 copy-done.3
  2.8 0.0 copy-start
  2.8 1.2 copy-done
  4.0 155.0 %shard_map.91 = bf16[64,64,128]{2,1,0:T(8,128)(2,1)S(1)} custom-call(bf16[64,64,128]{2,1,0:T(8,128)(2,1)S(1)} %copy-done, f32[32,128]{1,0:T(8,128)S(1)} %pad_maximum_fusion.mask_ref, f32[2,128]{1,0:T(2,128)S(1)} %copy-done.3, f32[2,128]{1,0:T(2,128)S(1)} %copy-done.4, bf16[2,512,128]{2,1,0:T(8,128)(2,1)S(1)} %bitcast.4, bf16[2,128,128]{2,1,0:T(8,128)(2,1)S(1)} %copy-done.1, ...), custom_call_target="tpu_custom_call" | custom-call | tf_op jit(solution)/shard_map/pallas_call | solution.py:394
  159.0 1.0 copy.15
  (1 shorter events, 0.0 us)
Async XLA Ops:
  0.0 1.9 %copy-start.5 = (bf16[2,128,4,128]{3,2,1,0:T(4,128)(2,1)S(1)}, bf16[2,128,4,128]{3,2,1,0:T(4,128)(2,1)}, u32[]{:S(2)}) copy-start(bf16[2,128,4,128]{3,2,1,0:T(4,128)(2,1)} %param.13) | copy-start | bytes 786436
  0.9 0.8 copy-start.6
  1.9 0.8 copy-start.1
  1.9 0.9 copy-start.2
  1.9 0.9 copy-start.4
  2.1 0.7 copy-start.3
  2.8 1.2 copy-start

commit v2 on v1

--- a/solution.py
+++ b/solution.py
@@ -135,6 +135,7 @@
 
 
 PARTS = 2
+GROUPS = 2
 UNROLL = 4
 
 
@@ -169,28 +170,39 @@
     right_wide,
     sum_wide,
     gate_buf,
-    edge_send,
-    edge_recv,
+    left_send,
+    right_send,
+    left_recv,
+    right_recv,
     sum_send,
     sum_recv,
-    edge_ssem,
-    edge_rsem,
+    left_ssem,
+    left_rsem,
+    right_ssem,
+    right_rsem,
     sum_ssem,
     sum_rsem,
 ):
+    owners = 2 * chan
     peers = rows * chan
     my_row = lax.axis_index("rows")
     my_chan = lax.axis_index("chan")
-    me = my_chan * rows + my_row
+    my_half = lax.div(my_row, 2)
+    slot = my_chan * 2 + lax.rem(my_row, 2)
+    me = my_half * owners + slot
     side = pair_ref.shape[1]
     width = pair_ref.shape[2]
     half = pair_ref.shape[0] // 2
-    own = edge_send.shape[4]
+    batch = left_send.shape[4]
     depth = half // PARTS
     lanes = 2 * side
 
     def coords(peer):
-        return {"rows": lax.rem(peer, rows), "chan": lax.div(peer, rows)}
+        place = lax.rem(peer, owners)
+        return {
+            "rows": 2 * lax.div(peer, owners) + lax.rem(place, 2),
+            "chan": lax.div(place, 2),
+        }
 
     barrier = pltpu.get_barrier_semaphore()
 
@@ -201,24 +213,59 @@
             barrier, inc=1, device_id=coords(peer), device_id_type=pl.DeviceIdType.MESH
         )
 
-    def edge_copy(u, part, step, peer):
+    def near(step):
+        return lax.rem(slot + step, owners)
+
+    def remote(src, dst, ssem, rsem, peer):
         return pltpu.make_async_remote_copy(
-            src_ref=edge_send.at[u, part, peer],
-            dst_ref=edge_recv.at[u, part, me],
-            send_sem=edge_ssem.at[u, part, step],
-            recv_sem=edge_rsem.at[u, part, step],
+            src_ref=src,
+            dst_ref=dst,
+            send_sem=ssem,
+            recv_sem=rsem,
             device_id=coords(peer),
             device_id_type=pl.DeviceIdType.MESH,
         )
 
-    def sum_copy(u, part, step, peer):
-        return pltpu.make_async_remote_copy(
-            src_ref=sum_send.at[u, part, peer],
-            dst_ref=sum_recv.at[u, part, me],
-            send_sem=sum_ssem.at[u, part, step],
-            recv_sem=sum_rsem.at[u, part, step],
-            device_id=coords(peer),
-            device_id_type=pl.DeviceIdType.MESH,
+    def left_copy(u, part, group, step):
+        where = (u, part, group)
+        if u == 0:
+            place, mine = near(step), slot
+            peer = my_half * owners + place
+        else:
+            peer, mine = lax.rem(me + step, peers), me
+            place = lax.rem(peer, owners)
+        return remote(
+            left_send.at[(*where, place)],
+            left_recv.at[(*where, mine)],
+            left_ssem.at[(*where, step)],
+            left_rsem.at[(*where, step)],
+            peer,
+        )
+
+    def right_copy(u, part, group, step):
+        where = (u, part, group)
+        return remote(
+            right_send.at[(*where, near(step))],
+            right_recv.at[(*where, slot)],
+            right_ssem.at[(*where, step)],
+            right_rsem.at[(*where, step)],
+            my_half * owners + near(step),
+        )
+
+    def sum_copy(u, part, group, step):
+        where = (u, part, group)
+        if u == 0:
+            place, mine = lax.rem(me + step, peers), me
+            peer = place
+        else:
+            place, mine = near(step), slot
+            peer = my_half * owners + place
+        return remote(
+            sum_send.at[(*where, place)],
+            sum_recv.at[(*where, mine)],
+            sum_ssem.at[(*where, step)],
+            sum_rsem.at[(*where, step)],
+            peer,
         )
 
     def make_edges(u, part, source):
@@ -243,51 +290,60 @@
                 jnp.dot(normed, gate_w_ref[u], preferred_element_type=jnp.float32)
             )
 
-    def narrow(wide, part, peer):
-        return wide[pl.ds(peer * own, own), part * depth : (part + 1) * depth, :].astype(
-            jnp.bfloat16
-        )
-
     def send_edges(u, part):
-        @pl.loop(1, peers)
+        piece = slice(part * depth, (part + 1) * depth)
+        for group in range(GROUPS):
+
+            @pl.loop(0, owners)
+            def _(place):
+                first = (place * GROUPS + group) * batch
+                left_send[u, part, group, place] = left_wide[
+                    pl.ds(first, batch), piece, :
+                ].astype(jnp.bfloat16)
+                right_send[u, part, group, place] = right_wide[
+                    pl.ds(first, batch), piece, :
+                ].astype(jnp.bfloat16)
+
+            @pl.loop(1, owners)
+            def _(step):
+                right_copy(u, part, group, step).start()
+
+            @pl.loop(1, owners if u == 0 else peers)
+            def _(step):
+                left_copy(u, part, group, step).start()
+
+            right_recv[u, part, group, slot] = right_send[u, part, group, slot]
+            left_recv[u, part, group, slot if u == 0 else me] = left_send[u, part, group, slot]
+
+    def wait_edges(u, part, group):
+        @pl.loop(1, owners)
         def _(step):
-            peer = lax.rem(me + step, peers)
-            edge_send[u, part, peer, 0] = narrow(left_wide, part, peer)
-            edge_send[u, part, peer, 1] = narrow(right_wide, part, peer)
-            edge_copy(u, part, step, peer).start()
-
-        edge_recv[u, part, me, 0] = narrow(left_wide, part, me)
-        edge_recv[u, part, me, 1] = narrow(right_wide, part, me)
-
-    def wait_edges(u, part):
-        @pl.loop(1, peers)
+            right_copy(u, part, group, step).wait()
+
+        @pl.loop(1, owners if u == 0 else peers)
         def _(step):
-            edge_copy(u, part, step, lax.rem(me + step, peers)).wait()
-
-    def make_sums(u):
-        @pl.loop(0, own, unroll=2)
+            left_copy(u, part, group, step).wait()
+
+    def make_sums(u, group):
+        @pl.loop(0, batch, unroll=2)
         def _(c):
-            def whole(kind):
+            def whole(edges, first):
                 pieces = []
                 for a in range(chan):
-                    first, second = [], []
-                    for r in range(0, rows, 2):
-                        low, high = (
-                            jnp.concatenate(
-                                [edge_recv[u, part, peer, kind, c] for part in range(PARTS)],
-                                axis=0,
-                            ).astype(jnp.float32)
-                            for peer in (a * rows + r, a * rows + r + 1)
-                        )
-                        one, two = swap_halves(low, high)
-                        first.append(one)
-                        second.append(two)
-                    pieces.append(jnp.concatenate(first, axis=1))
-                    pieces.append(jnp.concatenate(second, axis=1))
+                    low, high = (
+                        jnp.concatenate(
+                            [edges[u, part, group, place, c] for part in range(PARTS)], axis=0
+                        ).astype(jnp.float32)
+                        for place in (first + 2 * a, first + 2 * a + 1)
+                    )
+                    pieces.extend(swap_halves(low, high))
                 return jnp.concatenate(pieces, axis=0).astype(jnp.bfloat16)
 
-            left = whole(0)
-            right = whole(1)
+            if u == 0:
+                left = whole(left_recv, 0)
+            else:
+                left = jnp.concatenate([whole(left_recv, 0), whole(left_recv, owners)], axis=1)
+            right = whole(right_recv, 0)
             over = 1 if u == 0 else 0
             summed = lax.dot_general(
                 left,
@@ -296,32 +352,41 @@
                 preferred_element_type=jnp.float32,
             )
             for a in range(chan):
-                for r in range(0, rows, 2):
+                for tile in range(summed.shape[1] // lanes):
                     top = 2 * half * a
-                    upper = summed[top : top + half, r * side : r * side + lanes]
-                    lower = summed[top + half : top + 2 * half, r * side : r * side + lanes]
-                    one, two = swap_halves(upper, lower)
+                    columns = slice(tile * lanes, (tile + 1) * lanes)
+                    one, two = swap_halves(
+                        summed[top : top + half, columns],
+                        summed[top + half : top + 2 * half, columns],
+                    )
+                    place = tile * owners + 2 * a
                     for part in range(PARTS):
                         piece = slice(part * depth, (part + 1) * depth)
-                        sum_send[u, part, a * rows + r, c] = one[piece].astype(jnp.bfloat16)
-                        sum_send[u, part, a * rows + r + 1, c] = two[piece].astype(jnp.bfloat16)
-
-    def send_sums(u, part):
-        @pl.loop(1, peers)
+                        sum_send[u, part, group, place, c] = one[piece].astype(jnp.bfloat16)
+                        sum_send[u, part, group, place + 1, c] = two[piece].astype(jnp.bfloat16)
+
+    def send_sums(u, part, group):
+        @pl.loop(1, peers if u == 0 else owners)
         def _(step):
-            sum_copy(u, part, step, lax.rem(me + step, peers)).start()
+            sum_copy(u, part, group, step).start()
 
     def take_sums(u, part):
         piece = slice(part * depth, (part + 1) * depth)
-        sum_wide[pl.ds(me * own, own), piece, :] = sum_send[u, part, me].astype(jnp.float32)
-
-        @pl.loop(1, peers)
-        def _(step):
-            sum_copy(u, part, step, lax.rem(me + step, peers)).wait()
-            peer = lax.rem(me + peers - step, peers)
-            sum_wide[pl.ds(peer * own, own), piece, :] = sum_recv[u, part, peer].astype(
-                jnp.float32
-            )
+        mine = me if u == 0 else slot
+        for group in range(GROUPS):
+            sum_recv[u, part, group, mine] = sum_send[u, part, group, mine]
+
+            @pl.loop(1, peers if u == 0 else owners)
+            def _(step):
+                sum_copy(u, part, group, step).wait()
+
+            @pl.loop(0, owners)
+            def _(place):
+                total = sum_recv[u, part, group, place].astype(jnp.float32)
+                if u == 0:
+                    total += sum_recv[u, part, group, place + owners].astype(jnp.float32)
+                first = (place * GROUPS + group) * batch
+                sum_wide[pl.ds(first, batch), piece, :] = total
 
     def mix(u, part, source, target):
         @pl.loop(part * depth, (part + 1) * depth, unroll=UNROLL)
@@ -344,26 +409,26 @@
                 source[ip + half].astype(jnp.float32) + moved[side:]
             ).astype(jnp.bfloat16)
 
+    def sums_of(u):
+        for group in range(GROUPS):
+            for part in range(PARTS):
+                wait_edges(u, part, group)
+            make_sums(u, group)
+            for part in range(PARTS):
+                send_sums(u, part, group)
+
     for part in range(PARTS):
         make_edges(0, part, pair_ref)
         if part == 0:
             pl.semaphore_wait(barrier, peers - 1)
         send_edges(0, part)
-    for part in range(PARTS):
-        wait_edges(0, part)
-    make_sums(0)
-    for part in range(PARTS):
-        send_sums(0, part)
+    sums_of(0)
     for part in range(PARTS):
         take_sums(0, part)
         mix(0, part, pair_ref, mid_ref)
         make_edges(1, part, mid_ref)
         send_edges(1, part)
-    for part in range(PARTS):
-        wait_edges(1, part)
-    make_sums(1)
-    for part in range(PARTS):
-        send_sums(1, part)
+    sums_of(1)
     for part in range(PARTS):
         take_sums(1, part)
         mix(1, part, mid_ref, out_ref)
@@ -385,8 +450,9 @@
         half = first // 2
         hidden = proj_weight.shape[-1]
         peers = rows * chan
-        own = hidden // peers
+        owners = 2 * chan
         lanes = 2 * side
+        block = (hidden // owners // GROUPS, half // PARTS, lanes)
         mask_float = pair_mask.astype(jnp.float32)
         mask_rows = jnp.concatenate([mask_float[:half], mask_float[half:]], axis=1)
         proj_flat = jnp.transpose(proj_weight, (0, 2, 3, 1)).reshape(2, 4 * hidden, width)
@@ -402,14 +468,13 @@
                 pltpu.VMEM((hidden, half, lanes), jnp.float32),
                 pltpu.VMEM((hidden, half, lanes), jnp.float32),
                 pltpu.VMEM((2, half, lanes, width), jnp.float32),
-                pltpu.VMEM((2, PARTS, peers, 2, own, half // PARTS, lanes), jnp.bfloat16),
-                pltpu.VMEM((2, PARTS, peers, 2, own, half // PARTS, lanes), jnp.bfloat16),
-                pltpu.VMEM((2, PARTS, peers, own, half // PARTS, lanes), jnp.bfloat16),
-                pltpu.VMEM((2, PARTS, peers, own, half // PARTS, lanes), jnp.bfloat16),
-                pltpu.SemaphoreType.DMA((2, PARTS, peers)),
-                pltpu.SemaphoreType.DMA((2, PARTS, peers)),
-                pltpu.SemaphoreType.DMA((2, PARTS, peers)),
-                pltpu.SemaphoreType.DMA((2, PARTS, peers)),
+                pltpu.VMEM((2, PARTS, GROUPS, owners, *block), jnp.bfloat16),
+                pltpu.VMEM((2, PARTS, GROUPS, owners, *block), jnp.bfloat16),
+                pltpu.VMEM((2, PARTS, GROUPS, peers, *block), jnp.bfloat16),
+                pltpu.VMEM((2, PARTS, GROUPS, owners, *block), jnp.bfloat16),
+                pltpu.VMEM((2, PARTS, GROUPS, peers, *block), jnp.bfloat16),
+                pltpu.VMEM((2, PARTS, GROUPS, peers, *block), jnp.bfloat16),
+                *[pltpu.SemaphoreType.DMA((2, PARTS, GROUPS, peers))] * 6,
             ],
             compiler_params=pltpu.CompilerParams(
                 collective_id=0, has_side_effects=True, vmem_limit_bytes=48 * 1024 * 1024
@@ -450,8 +515,8 @@
         fits = (
             pair_act.shape[1] == 64
             and pair_act.shape[0] % (32 * PARTS) == 0
-            and rows % 2 == 0
-            and hidden % (rows * chan) == 0
+            and rows == 4
+            and hidden % (2 * chan * GROUPS) == 0
         )
         body = fused if fits else on_device
         return body(pair_act, pair_mask, *parameters)

time: 160 us -> 148 us (0.925)
  Pallas kernels: 155 us -> 143 us
    pallas_call x1, Pallas kernels: 155 us -> 143 us  [run(): pl.pallas_call(functools.partial(fused_kernel, rows, chan), out_shape=jax...]
where the time goes in v2:
time: 148 us
  Pallas kernels  143 us (97%)
  local copies, waits for them, and re-layouts  4.06 us (3%)
    pallas_call x1, Pallas kernels, run(): pl.pallas_call(functools.partial(fused_kernel, rows, chan), out_shape=jax...  143 us

profile of v2, /device:TPU:0, one launch (start us, length us, event | category | flops | bytes accessed | tf_op | source)
XLA Modules:
  0.0 147.6 jit_solution(550364448577768579)
XLA Ops:
  0.0 0.0 copy-start.5
  0.0 0.8 convert_element_type.3
  0.8 0.1 pad_maximum_fusion.mask_ref
  0.9 0.0 copy-start.6
  0.9 0.8 copy.12.out_gain_ref
  1.7 0.0 copy-done.6
  1.7 0.1 copy.13.out_bias_ref
  1.9 0.0 copy-done.5
  1.9 0.0 copy-start.1
  1.9 0.0 copy-start.2
  1.9 0.0 copy-start.4
  1.9 0.2 copy.11
  2.1 0.0 copy-start.3
  2.1 0.6 copy-done.1
  2.7 0.0 copy-done.2
  2.8 0.0 copy-done.4
  2.8 0.1 copy-done.3
  2.8 0.0 copy-start
  2.8 1.2 copy-done
  4.0 142.6 %shard_map.91 = bf16[64,64,128]{2,1,0:T(8,128)(2,1)S(1)} custom-call(bf16[64,64,128]{2,1,0:T(8,128)(2,1)S(1)} %copy-done, f32[32,128]{1,0:T(8,128)S(1)} %pad_maximum_fusion.mask_ref, f32[2,128]{1,0:T(2,128)S(1)} %copy-done.3, f32[2,128]{1,0:T(2,128)S(1)} %copy-done.4, bf16[2,512,128]{2,1,0:T(8,128)(2,1)S(1)} %bitcast.4, bf16[2,128,128]{2,1,0:T(8,128)(2,1)S(1)} %copy-done.1, ...), custom_call_target="tpu_custom_call" | custom-call | tf_op jit(solution)/shard_map/pallas_call | solution.py:460
  146.6 1.0 copy.15
  (1 shorter events, 0.0 us)
Async XLA Ops:
  0.0 1.9 %copy-start.5 = (bf16[2,128,4,128]{3,2,1,0:T(4,128)(2,1)S(1)}, bf16[2,128,4,128]{3,2,1,0:T(4,128)(2,1)}, u32[]{:S(2)}) copy-start(bf16[2,128,4,128]{3,2,1,0:T(4,128)(2,1)} %param.13) | copy-start | bytes 786436
  0.9 0.8 copy-start.6
  1.9 0.8 copy-start.1
  1.9 0.9 copy-start.2
  1.9 0.9 copy-start.4
  2.1 0.7 copy-start.3
  2.8 1.2 copy-start

commit v3 on v2

--- a/solution.py
+++ b/solution.py
@@ -170,6 +170,9 @@
     right_wide,
     sum_wide,
     gate_buf,
+    normed_buf,
+    mask_buf,
+    column_buf,
     left_send,
     right_send,
     left_recv,
@@ -268,52 +271,65 @@
             peer,
         )
 
-    def make_edges(u, part, source):
+    def norm_cells(u, part, source):
         @pl.loop(part * depth, (part + 1) * depth, unroll=UNROLL)
         def _(ip):
             cells = jnp.concatenate([source[ip], source[ip + half]], axis=0).astype(jnp.float32)
             center = cells - jnp.mean(cells, axis=-1, keepdims=True)
             spread = jnp.mean(center * center, axis=-1, keepdims=True)
-            normed = (
+            normed_buf[ip] = (
                 center * lax.rsqrt(spread + 1e-05) * in_gain_ref[u : u + 1, :]
                 + in_bias_ref[u : u + 1, :]
             ).astype(jnp.bfloat16)
+
+    def make_gates(u):
+        @pl.loop(0, half, unroll=UNROLL)
+        def _(ip):
+            gate_buf[ip] = sigmoid(
+                jnp.dot(normed_buf[ip], gate_w_ref[u], preferred_element_type=jnp.float32)
+            )
+
+    def make_edges(u, part, group):
+        count = width // GROUPS
+        first = group * count
+
+        @pl.loop(part * depth, (part + 1) * depth, unroll=UNROLL)
+        def _(ip):
             projected = lax.dot_general(
-                proj_ref[u], normed, (((1,), (1,)), ((), ())), preferred_element_type=jnp.float32
-            )
-            mask_row = mask_ref[pl.ds(ip, 1), :]
-            left = sigmoid(projected[width : 2 * width]) * projected[:width] * mask_row
-            right = sigmoid(projected[3 * width :]) * projected[2 * width : 3 * width] * mask_row
-            left_wide[:, pl.ds(ip, 1), :] = left[:, None, :]
-            right_wide[:, pl.ds(ip, 1), :] = right[:, None, :]
-            gate_buf[u, ip] = sigmoid(
-                jnp.dot(normed, gate_w_ref[u], preferred_element_type=jnp.float32)
-            )
-
-    def send_edges(u, part):
+                proj_ref[u, group],
+                normed_buf[ip],
+                (((1,), (1,)), ((), ())),
+                preferred_element_type=jnp.float32,
+            )
+            mask_row = mask_buf[pl.ds(ip, 1), :]
+            left = sigmoid(projected[count : 2 * count]) * projected[:count] * mask_row
+            right = sigmoid(projected[3 * count :]) * projected[2 * count : 3 * count] * mask_row
+            left_wide[first : first + count, pl.ds(ip, 1), :] = left[:, None, :]
+            right_wide[first : first + count, pl.ds(ip, 1), :] = right[:, None, :]
+
+    def send_edges(u, part, group):
         piece = slice(part * depth, (part + 1) * depth)
-        for group in range(GROUPS):
-
-            @pl.loop(0, owners)
-            def _(place):
-                first = (place * GROUPS + group) * batch
-                left_send[u, part, group, place] = left_wide[
-                    pl.ds(first, batch), piece, :
-                ].astype(jnp.bfloat16)
-                right_send[u, part, group, place] = right_wide[
-                    pl.ds(first, batch), piece, :
-                ].astype(jnp.bfloat16)
-
-            @pl.loop(1, owners)
-            def _(step):
-                right_copy(u, part, group, step).start()
-
-            @pl.loop(1, owners if u == 0 else peers)
-            def _(step):
-                left_copy(u, part, group, step).start()
-
-            right_recv[u, part, group, slot] = right_send[u, part, group, slot]
-            left_recv[u, part, group, slot if u == 0 else me] = left_send[u, part, group, slot]
+
+        @pl.loop(0, owners)
+        def _(place):
+            first = (group * owners + place) * batch
+            left_send[u, part, group, place] = left_wide[pl.ds(first, batch), piece, :].astype(
+                jnp.bfloat16
+            )
+            right_send[u, part, group, place] = right_wide[pl.ds(first, batch), piece, :].astype(
+                jnp.bfloat16
+            )
+
+        @pl.loop(1, owners if u == 0 else peers)
+        def _(step):
+            left_copy(u, part, group, step).start()
+
+        @pl.loop(1, owners)
+        def _(step):
+            right_copy(u, part, group, step).start()
+
+        right_recv[u, part, group, slot] = right_send[u, part, group, slot]
+        left_recv[u, part, group, slot if u == 0 else me] = left_send[u, part, group, slot]
 
     def wait_edges(u, part, group):
         @pl.loop(1, owners)
@@ -385,7 +401,7 @@
                 total = sum_recv[u, part, group, place].astype(jnp.float32)
                 if u == 0:
                     total += sum_recv[u, part, group, place + owners].astype(jnp.float32)
-                first = (place * GROUPS + group) * batch
+                first = (group * owners + place) * batch
                 sum_wide[pl.ds(first, batch), piece, :] = total
 
     def mix(u, part, source, target):
@@ -395,7 +411,7 @@
             center = values - jnp.mean(values, axis=0, keepdims=True)
             spread = jnp.mean(center * center, axis=0, keepdims=True)
             normed = (
-                center * lax.rsqrt(spread + 1e-05) * out_gain_ref[u] + out_bias_ref[u]
+                center * lax.rsqrt(spread + 1e-05) * column_buf[0, u] + column_buf[1, u]
             ).astype(jnp.bfloat16)
             mixed = lax.dot_general(
                 normed,
@@ -403,7 +419,7 @@
                 (((0,), (0,)), ((), ())),
                 preferred_element_type=jnp.float32,
             )
-            moved = gate_buf[u, ip] * mixed
+            moved = gate_buf[ip] * mixed
             target[ip] = (source[ip].astype(jnp.float32) + moved[:side]).astype(jnp.bfloat16)
             target[ip + half] = (
                 source[ip + half].astype(jnp.float32) + moved[side:]
@@ -417,17 +433,31 @@
             for part in range(PARTS):
                 send_sums(u, part, group)
 
-    for part in range(PARTS):
-        make_edges(0, part, pair_ref)
-        if part == 0:
-            pl.semaphore_wait(barrier, peers - 1)
-        send_edges(0, part)
+    mask_buf[:, :side] = mask_ref[:half].astype(jnp.float32)
+    mask_buf[:, side:] = mask_ref[half:].astype(jnp.float32)
+    for group in range(GROUPS):
+        for part in range(PARTS):
+            if group == 0:
+                norm_cells(0, part, pair_ref)
+            make_edges(0, part, group)
+            if group == 0 and part == 0:
+                pl.semaphore_wait(barrier, peers - 1)
+            send_edges(0, part, group)
+    for index, vector in enumerate((out_gain_ref, out_bias_ref)):
+        for u in range(2):
+            column_buf[index, u] = jnp.transpose(
+                jnp.broadcast_to(vector[u : u + 1, :], (lanes, width))
+            )
+    make_gates(0)
     sums_of(0)
     for part in range(PARTS):
         take_sums(0, part)
         mix(0, part, pair_ref, mid_ref)
-        make_edges(1, part, mid_ref)
-        send_edges(1, part)
+        norm_cells(1, part, mid_ref)
+        for group in range(GROUPS):
+            make_edges(1, part, group)
+            send_edges(1, part, group)
+    make_gates(1)
     sums_of(1)
     for part in range(PARTS):
         take_sums(1, part)
@@ -453,9 +483,10 @@
         owners = 2 * chan
         lanes = 2 * side
         block = (hidden // owners // GROUPS, half // PARTS, lanes)
-        mask_float = pair_mask.astype(jnp.float32)
-        mask_rows = jnp.concatenate([mask_float[:half], mask_float[half:]], axis=1)
-        proj_flat = jnp.transpose(proj_weight, (0, 2, 3, 1)).reshape(2, 4 * hidden, width)
+        grouped = proj_weight.reshape(2, width, 4, GROUPS, hidden // GROUPS)
+        proj_flat = jnp.transpose(grouped, (0, 3, 2, 4, 1)).reshape(
+            2, GROUPS, 4 * hidden // GROUPS, width
+        )
         vmem = pl.BlockSpec(memory_space=pltpu.VMEM)
         return pl.pallas_call(
             functools.partial(fused_kernel, rows, chan),
@@ -467,7 +498,10 @@
                 pltpu.VMEM((hidden, half, lanes), jnp.float32),
                 pltpu.VMEM((hidden, half, lanes), jnp.float32),
                 pltpu.VMEM((hidden, half, lanes), jnp.float32),
-                pltpu.VMEM((2, half, lanes, width), jnp.float32),
+                pltpu.VMEM((half, lanes, width), jnp.float32),
+                pltpu.VMEM((half, lanes, width), jnp.bfloat16),
+                pltpu.VMEM((half, lanes), jnp.float32),
+                pltpu.VMEM((2, 2, hidden, lanes), jnp.float32),
                 pltpu.VMEM((2, PARTS, GROUPS, owners, *block), jnp.bfloat16),
                 pltpu.VMEM((2, PARTS, GROUPS, owners, *block), jnp.bfloat16),
                 pltpu.VMEM((2, PARTS, GROUPS, peers, *block), jnp.bfloat16),
@@ -481,13 +515,13 @@
             ),
         )(
             pair_act,
-            mask_rows,
+            pair_mask,
             input_gain,
             input_bias,
             proj_flat,
             gate_weight,
-            output_gain[:, :, None],
-            output_bias[:, :, None],
+            output_gain,
+            output_bias,
             out_weight,
         )
 

time: 148 us -> 138 us (0.932)
  Pallas kernels: 143 us -> 132 us
  local copies, waits for them, and re-layouts: 4.06 us -> 6.01 us
    pallas_call x1, Pallas kernels: 143 us -> 132 us  [run(): pl.pallas_call(functools.partial(fused_kernel, rows, chan), out_shape=jax...]
    unnamed x15 -> x18, local copies, waits for them, and re-layouts: 2.91 us -> 5.99 us
where the time goes in v3:
time: 138 us
  Pallas kernels  132 us (96%)
  local copies, waits for them, and re-layouts  6.01 us (4%)
    pallas_call x1, Pallas kernels, run(): pl.pallas_call(functools.partial(fused_kernel, rows, chan), out_shape=jax...  132 us
    unnamed x18, local copies, waits for them, and re-layouts  5.99 us

profile of v3, /device:TPU:0, one launch (start us, length us, event | category | flops | bytes accessed | tf_op | source)
XLA Modules:
  0.0 137.7 jit_solution(1381447958580817435)
XLA Ops:
  0.0 0.0 copy-start
  0.0 1.2 copy.11
  1.2 0.0 copy-start.5
  1.2 0.0 copy-start.6
  1.3 0.0 copy-start.4
  1.3 0.0 copy-done
  1.3 0.6 copy-done.5
  1.9 0.0 copy-done.6
  1.9 0.0 copy-done.4
  2.0 0.0 copy-start.1
  2.0 0.8 copy-done.1
  2.8 0.0 copy-start.2
  2.8 0.8 copy-done.2
  3.6 0.0 copy-start.3
  3.6 0.8 copy-done.3
  4.4 0.0 copy-start.7
  4.4 0.7 copy-done.7
  5.1 131.6 %shard_map.91 = bf16[64,64,128]{2,1,0:T(8,128)(2,1)S(1)} custom-call(bf16[64,64,128]{2,1,0:T(8,128)(2,1)S(1)} %copy-done, s32[64,64]{1,0:T(8,128)S(1)} %copy-done.3, f32[2,128]{1,0:T(2,128)S(1)} %copy-done.4, f32[2,128]{1,0:T(2,128)S(1)} %copy-done.5, bf16[2,2,256,128]{3,2,1,0:T(8,128)(2,1)S(1)} %bitcast.4, bf16[2,128,128]{2,1,0:T(8,128)(2,1)S(1)} %copy-done.1, ...), custom_call_target="tpu_custom_call" | custom-call | tf_op jit(solution)/shard_map/pallas_call | solution.py:491
  136.7 1.0 copy.14
  (1 shorter events, 0.0 us)
Async XLA Ops:
  0.0 1.3 copy-start
  1.2 0.7 copy-start.5
  1.2 0.7 copy-start.6
  1.3 0.7 copy-start.4
  2.0 0.8 copy-start.1
  2.8 0.8 copy-start.2
  3.6 0.8 copy-start.3
  4.4 0.7 copy-start.7

commit v4 on v3

--- a/solution.py
+++ b/solution.py
@@ -136,7 +136,7 @@
 
 PARTS = 2
 GROUPS = 2
-UNROLL = 4
+UNROLL = 8
 
 
 def sigmoid(values):

time: 138 us -> 137 us (level)
  no operation moved by 1% of the time
where the time goes in v4:
time: 137 us
  Pallas kernels  131 us (96%)
  local copies, waits for them, and re-layouts  6.01 us (4%)
    pallas_call x1, Pallas kernels, run(): pl.pallas_call(functools.partial(fused_kernel, rows, chan), out_shape=jax...  131 us
    unnamed x18, local copies, waits for them, and re-layouts  5.99 us

profile of v4, /device:TPU:0, one launch (start us, length us, event | category | flops | bytes accessed | tf_op | source)
XLA Modules:
  0.0 137.0 jit_solution(9840293021977439577)
XLA Ops:
  0.0 0.0 copy-start
  0.0 1.2 copy.11
  1.2 0.0 copy-start.5
  1.2 0.0 copy-start.6
  1.3 0.0 copy-start.4
  1.3 0.0 copy-done
  1.3 0.6 copy-done.5
  1.9 0.0 copy-done.6
  1.9 0.0 copy-done.4
  2.0 0.0 copy-start.1
  2.0 0.8 copy-done.1
  2.8 0.0 copy-start.2
  2.8 0.8 copy-done.2
  3.6 0.0 copy-start.3
  3.6 0.8 copy-done.3
  4.4 0.0 copy-start.7
  4.4 0.7 copy-done.7
  5.1 131.0 %shard_map.91 = bf16[64,64,128]{2,1,0:T(8,128)(2,1)S(1)} custom-call(bf16[64,64,128]{2,1,0:T(8,128)(2,1)S(1)} %copy-done, s32[64,64]{1,0:T(8,128)S(1)} %copy-done.3, f32[2,128]{1,0:T(2,128)S(1)} %copy-done.4, f32[2,128]{1,0:T(2,128)S(1)} %copy-done.5, bf16[2,2,256,128]{3,2,1,0:T(8,128)(2,1)S(1)} %bitcast.4, bf16[2,128,128]{2,1,0:T(8,128)(2,1)S(1)} %copy-done.1, ...), custom_call_target="tpu_custom_call" | custom-call | tf_op jit(solution)/shard_map/pallas_call | solution.py:491
  136.0 1.0 copy.14
  (1 shorter events, 0.0 us)
Async XLA Ops:
  0.0 1.3 copy-start
  1.2 0.7 copy-start.5
  1.2 0.7 copy-start.6
  1.3 0.7 copy-start.4
  2.0 0.8 copy-start.1
  2.8 0.8 copy-start.2
  3.6 0.8 copy-start.3
  4.4 0.7 copy-start.7
